TPU v7x, 32 devices: a whole 2x2x4 slice. The times are simulated.
32 devices in a mesh: pipe: 4 (over y, core), node: 4 (over z), ep: 2 (over x).
Axes of the slice: x: 2, y: 2, z: 4, core: 2. Of those that a mesh axis runs over, the one named last changes fastest.
Arguments:
- grad_tokens: bfloat16 [4, 4, 2, 128, 7168], P('pipe', 'node', 'ep'), may hold values from -6 to 6
- slot_token: int32 [4, 4, 2, 4, 8], P('pipe', 'node', 'ep'), may hold values from 0 to 127, as said below
- send_count: int32 [4, 4, 2, 4], P('pipe', 'node', 'ep'), may hold values from 1 to 8, as said below
- route_score: float32 [4, 4, 2, 4, 8], P('pipe', 'node', 'ep'), may hold values from 0.05 to 1
- hidden_act: bfloat16 [4, 4, 64, 1024], P('pipe', 'node', 'ep'), may hold values from -2.390625 to 2.390625
- w_down: bfloat16 [4, 4, 1024, 7168], P('pipe', 'node', None, 'ep'), as said below
Outputs:
- grad_hidden: bfloat16 [4, 4, 64, 1024], P('pipe', 'node', 'ep')
- grad_weight: bfloat16 [4, 4, 512, 7168], P('pipe', 'node', None, 'ep')
Inputs may be any that keep to these rules, and one draw needn't show every extreme that they name: `slot_token`: the 8 entries for one device and one node group are distinct tokens of that device; only the first send_count of them are sent. `send_count`: in every section one node group, drawn from the seed, receives 8 rows from every device of the section; every other count is at most 5. w_down[p] equals w_down[3 - p].
All inputs are finite; a program needn't handle non-finite values.
Results may differ from a plain program's by a relative error of at most 0.0059.
Values may be sent and summed in bfloat16 or wider, within the bound.
A program may use at most 128 MiB of HBM per device.

v0:
```python
import jax
import jax.numpy as jnp
from jax import lax
from jax.sharding import PartitionSpec as P


def partner(value, axis, bit):
    mask = 2**bit
    pairs = [(source, source ^ mask) for source in range(lax.axis_size(axis))]
    return lax.ppermute(value, axis, pairs)


def mirror_sum(weight_part):
    sections = lax.axis_size("pipe")
    section_index = lax.axis_index("pipe")
    half_rows = weight_part.shape[0] // 2
    is_lower = section_index < sections // 2
    keep_first = jnp.where(is_lower, 0, half_rows).astype(jnp.int32)
    give_first = jnp.where(is_lower, half_rows, 0).astype(jnp.int32)
    kept_half = lax.dynamic_slice_in_dim(weight_part, keep_first, half_rows, 0)
    given_half = lax.dynamic_slice_in_dim(weight_part, give_first, half_rows, 0)
    for bit_level in range(sections.bit_length() - 1):
        given_half = partner(given_half, "pipe", bit_level)
    return (kept_half.astype(jnp.float32) + given_half.astype(jnp.float32)).astype(jnp.bfloat16)


def local(grad_tokens, slot_token, send_count, route_score, hidden_act, w_down):
    tokens = grad_tokens[0, 0, 0]
    slots = slot_token[0, 0, 0]
    counts = send_count[0, 0, 0]
    scores = route_score[0, 0, 0]
    groups = lax.axis_size("node")
    owners = lax.axis_size("ep")
    tok_rows, feature_width = tokens.shape
    capacity = slots.shape[1]
    slice_width = feature_width // owners
    flat_rows = tokens.reshape(tok_rows * owners, slice_width)
    lane_ids = jnp.arange(owners, dtype=jnp.int32)
    picked = slots[:, None, :] * owners + lane_ids[None, :, None]
    live_slots = jnp.arange(capacity, dtype=jnp.int32)[None, :] < counts[:, None]
    weights = jnp.where(live_slots, scores, 0.0)
    routed = (flat_rows[picked].astype(jnp.float32) * weights[:, None, :, None]).astype(
        jnp.bfloat16
    )
    arrived = lax.all_to_all(
        routed.reshape(groups * owners, capacity, slice_width),
        ("node", "ep"),
        split_axis=0,
        concat_axis=0,
        tiled=True,
    )
    arrived = arrived.reshape(-1, slice_width)
    weight_slice = w_down[0, 0]
    own_hidden = hidden_act[0, 0]
    row_block = arrived
    summed = lax.psum_scatter(
        lax.dot_general(
            row_block, weight_slice, (((1,), (1,)), ((), ())), preferred_element_type=jnp.float32
        ),
        "ep",
        scatter_dimension=0,
        tiled=True,
    )
    grad_hidden = summed.astype(jnp.bfloat16)
    row_block = arrived
    running = lax.dot_general(
        lax.all_gather(own_hidden, "ep", axis=0, tiled=True),
        row_block,
        (((0,), (0,)), ((), ())),
        preferred_element_type=jnp.float32,
    )
    grad_weight = mirror_sum(running.astype(jnp.bfloat16))
    return (grad_hidden[None, None], grad_weight[None, None])


def solution(mesh):
    in_specs = (
        P("pipe", "node", "ep", None, None),
        P("pipe", "node", "ep", None, None),
        P("pipe", "node", "ep", None),
        P("pipe", "node", "ep", None, None),
        P("pipe", "node", "ep", None),
        P("pipe", "node", None, "ep"),
    )
    out_specs = (P("pipe", "node", "ep", None), P("pipe", "node", None, "ep"))
    return jax.shard_map(local, mesh=mesh, in_specs=in_specs, out_specs=out_specs, check_vma=False)
```

profile of v0, /device:TPU:0, one launch (start us, length us, event | category | flops | bytes accessed | tf_op | source)
XLA Modules:
  0.0 146.2 jit_solution(3424213316111750866)
XLA Ops:
  7.2 0.0 copy-start.1
  7.2 0.7 multiply_bitcast_fusion
  7.9 0.1 reshape.68
  8.0 2.7 %reshape_squeeze.3 = bf16[256,3584]{1,0:T(8,128)(2,1)S(1)} reshape(bf16[1,1,1,128,7168]{4,3,2,1,0:T(8,128)(2,1)} %param.6) | data formatting | bytes 3670016 | tf_op jit(solution)/shard_map/reshape;squeeze | solution.py:37
  10.7 0.8 bitcast_select_fusion
  11.4 0.8 gather_fusion
  12.3 0.9 fusion.4
  13.2 7.3 %all-to-all-start = ((bf16[8,8,3584]{2,1,0:T(8,128)(2,1)}), bf16[8,8,3584]{2,1,0:T(8,128)(2,1)S(1)}, u32[]{:S(2)}, u32[]{:S(2)}) async-start(bf16[8,8,3584]{2,1,0:T(8,128)(2,1)} %fusion.4), calls=%async_computation | async-start | bytes 917504 | tf_op jit(solution)/shard_map/all_to_all | solution.py:45
  20.4 0.0 reduce-scatter.2.cloned.1.call-start
  20.5 0.0 copy-done.1
  20.5 7.1 %all-gather = bf16[1,1,64,1024]{3,2,1,0:T(8,128)(2,1)S(1)} all-gather(bf16[1,1,32,1024]{3,2,1,0:T(8,128)(2,1)S(1)} %copy-done.1), channel_id=2, replica_groups=mesh['pipe'=4,'node'=4,'ep'=2] {'ep'}, dimensions={2}, use_global_device_ids=true | all-gather | bytes 196608 | tf_op jit(solution)/shard_map/all_gather | solution.py:67
  27.6 5.9 %all-to-all-done = bf16[8,8,3584]{2,1,0:T(8,128)(2,1)S(1)} async-done(((bf16[8,8,3584]{2,1,0:T(8,128)(2,1)}), bf16[8,8,3584]{2,1,0:T(8,128)(2,1)S(1)}, u32[]{:S(2)}, u32[]{:S(2)}) %all-to-all-start) | async-done | bytes 458784 | tf_op jit(solution)/shard_map/all_to_all | solution.py:45
  33.5 2.1 %convolution_convert_fusion = bf16[3584,1024]{1,0:T(8,128)(2,1)S(1)} fusion(bf16[8,8,3584]{2,1,0:T(8,128)(2,1)S(1)} %all-to-all-done, bf16[1,1,64,1024]{3,2,1,0:T(8,128)(2,1)S(1)} %all-gather), kind=kOutput, calls=%fused_computation.1 | convolution fusion | flops 473432064 | bytes 7929856 | tf_op jit(solution)/shard_map/dot_general | solution.py:66
  35.6 0.0 copy-start
  35.6 2.9 %copy-done = bf16[3584,1024]{1,0:T(8,128)(2,1)} copy-done((bf16[3584,1024]{1,0:T(8,128)(2,1)}, bf16[3584,1024]{1,0:T(8,128)(2,1)S(1)}, u32[]{:S(2)}) %copy-start) | copy-done | bytes 7340056
  38.6 0.4 dynamic-slice_bitcast_fusion
  39.0 0.1 collective-permute-start
  39.1 6.5 %collective-permute-done = bf16[512,3584]{0,1:T(8,128)(2,1)} collective-permute-done((bf16[512,3584]{0,1:T(8,128)(2,1)S(1)}, bf16[512,3584]{0,1:T(8,128)(2,1)}, u32[]{:S(2)}, u32[]{:S(2)}) %collective-permute-start) | collective-permute-done | bytes 3670048 | tf_op jit(solution)/shard_map/ppermute | solution.py:10
  45.6 1.5 %collective-permute-start.1 = (bf16[512,3584]{0,1:T(8,128)(2,1)}, bf16[512,3584]{0,1:T(8,128)(2,1)}, u32[]{:S(2)}, u32[]{:S(2)}) collective-permute-start(bf16[512,3584]{0,1:T(8,128)(2,1)} %collective-permute-done), channel_id=1, source_target_pairs={{0,16},{8,24},{16,0},{24,8},{1,17},{9,25},{17,1},{25,9},{2,18},{10... | collective-permute-start | bytes 11010056 | tf_op jit(solution)/shard_map/ppermute | solution.py:10
  47.1 6.1 %fusion.1 = f32[64,1024]{1,0:T(8,128)} fusion(bf16[1,1,1024,3584]{3,2,1,0:T(8,128)(2,1)} %param.11, bf16[8,8,3584]{2,1,0:T(8,128)(2,1)S(1)} %all-to-all-done), kind=kOutput, calls=%fused_computation.4 | convolution fusion | flops 469762048 | bytes 8060928 | tf_op jit(solution)/shard_map/dot_general | solution.py:57
  53.2 0.0 reduce-scatter.2.cloned.1.call-update
  53.3 9.9 %reduce-scatter.2.cloned.1.call-done = f32[32,1024]{1,0:T(8,128)} async-done(((f32[64,1024]{1,0:T(8,128)}), f32[32,1024]{1,0:T(8,128)}) %reduce-scatter.2.cloned.1.call-update) | async-done | bytes 131088 | tf_op jit(solution)/shard_map/reduce_scatter | solution.py:56
  63.2 1.5 %convert_bitcast_fusion = bf16[1,1,32,1024]{3,2,1,0:T(8,128)(2,1)} fusion(f32[32,1024]{1,0:T(8,128)} %reduce-scatter.2.cloned.1.call-done), kind=kLoop, calls=%fused_computation.13 | loop fusion | flops 32768 | bytes 196608 | tf_op jit(solution)/shard_map/broadcast_in_dim | solution.py:73
  64.7 62.6 %collective-permute-done.1 = bf16[512,3584]{0,1:T(8,128)(2,1)} collective-permute-done((bf16[512,3584]{0,1:T(8,128)(2,1)}, bf16[512,3584]{0,1:T(8,128)(2,1)}, u32[]{:S(2)}, u32[]{:S(2)}) %collective-permute-start.1) | collective-permute-done | bytes 3670048 | tf_op jit(solution)/shard_map/ppermute | solution.py:10
  127.3 6.1 %fusion.3 = bf16[1,1,512,3584]{2,3,1,0:T(8,128)(2,1)} fusion(bf16[512,3584]{0,1:T(8,128)(2,1)} %collective-permute-done.1, bf16[3584,1024]{1,0:T(8,128)(2,1)} %copy-done, s32[]{:T(128)S(6)} %select_n.29), kind=kLoop, calls=%fused_computation.6 | loop fusion | flops 7340032 | bytes 11010052 | tf_op jit(solution)/shard_map/broadcast_in_dim | solution.py:73
  133.4 5.9 %copy.8 = bf16[1,1,512,3584]{3,2,1,0:T(8,128)(2,1)} copy(bf16[1,1,512,3584]{2,3,1,0:T(8,128)(2,1)} %fusion.3) | data formatting | bytes 7340032
  (3 shorter events, 0.0 us)
Async XLA Ops:
  7.2 13.3 %copy-start.1 = (bf16[1,1,32,1024]{3,2,1,0:T(8,128)(2,1)S(1)}, bf16[1,1,32,1024]{3,2,1,0:T(8,128)(2,1)}, u32[]{:S(2)}) copy-start(bf16[1,1,32,1024]{3,2,1,0:T(8,128)(2,1)} %param.10) | copy-start | bytes 196612
  13.2 20.3 %all-to-all-start = ((bf16[8,8,3584]{2,1,0:T(8,128)(2,1)}), bf16[8,8,3584]{2,1,0:T(8,128)(2,1)S(1)}, u32[]{:S(2)}, u32[]{:S(2)}) async-start(bf16[8,8,3584]{2,1,0:T(8,128)(2,1)} %fusion.4), calls=%async_computation | async-start | bytes 917504 | tf_op jit(solution)/shard_map/all_to_all | solution.py:45
  20.4 42.8 %reduce-scatter.2.cloned.1.call-start = ((), (), s32[]{:S(2)}) async-start(), calls=%async_computation.2 | async-start | bytes 393216 | tf_op jit(solution)/shard_map/reduce_scatter | solution.py:56
  35.6 3.0 %copy-start = (bf16[3584,1024]{1,0:T(8,128)(2,1)}, bf16[3584,1024]{1,0:T(8,128)(2,1)S(1)}, u32[]{:S(2)}) copy-start(bf16[3584,1024]{1,0:T(8,128)(2,1)S(1)} %convolution_convert_fusion) | copy-start | bytes 22020100
  39.0 6.6 %collective-permute-start = (bf16[512,3584]{0,1:T(8,128)(2,1)S(1)}, bf16[512,3584]{0,1:T(8,128)(2,1)}, u32[]{:S(2)}, u32[]{:S(2)}) collective-permute-start(bf16[512,3584]{0,1:T(8,128)(2,1)S(1)} %dynamic-slice_bitcast_fusion), channel_id=1, source_target_pairs={{0,8},{8,0},{16,24},{24,16},{1,9},{9,1},{17,25},{25,17},{2,10},{10... | collective-permute-start | bytes 11010056 | tf_op jit(solution)/shard_map/ppermute | solution.py:10
  45.6 81.7 %collective-permute-start.1 = (bf16[512,3584]{0,1:T(8,128)(2,1)}, bf16[512,3584]{0,1:T(8,128)(2,1)}, u32[]{:S(2)}, u32[]{:S(2)}) collective-permute-start(bf16[512,3584]{0,1:T(8,128)(2,1)} %collective-permute-done), channel_id=1, source_target_pairs={{0,16},{8,24},{16,0},{24,8},{1,17},{9,25},{17,1},{25,9},{2,18},{10... | collective-permute-start | bytes 11010056 | tf_op jit(solution)/shard_map/ppermute | solution.py:10
Sparse Core Ops, SparseCore 0:
  53.4 9.7 reduce-scatter.1
where the time goes:
time: 147 us; the launch traced here: 146 us
  waiting for transfers between devices  84.9 us (58%)
  between operations  14.1 us (10%)
  local copies, waits for them, and re-layouts  12.9 us (9%)
  other arithmetic  10 us (7%)
  starting transfers between devices  8.88 us (6%)
  matrix products  8.19 us (6%)
  blocking collectives  7.14 us (5%)
    ppermute x2, waiting for transfers between devices, partner(): return lax.ppermute(value, axis, pairs)  69.1 us
    reduce_scatter x1, waiting for transfers between devices, local(): lax.psum_scatter(lax.dot_general(row_block, weight_slice, (((1,), (1,)),...  9.93 us
    unnamed x5, local copies, waits for them, and re-layouts  8.86 us
    broadcast_in_dim x2, other arithmetic, local(): return (grad_hidden[None, None], grad_weight[None, None])  7.64 us
    all_to_all x1, starting transfers between devices, local(): lax.all_to_all(routed.reshape(groups * owners, capacity, slice_width), ('...  7.25 us
    all_gather x1, blocking collectives, local(): lax.all_gather(own_hidden, 'ep', axis=0, tiled=True)  7.14 us
    dot_general x1, matrix products, local(): lax.dot_general(row_block, weight_slice, (((1,), (1,)), ((), ())), prefer...  6.1 us
    all_to_all x1, waiting for transfers between devices, local(): lax.all_to_all(routed.reshape(groups * owners, capacity, slice_width), ('...  5.87 us
  transfers between devices with their start and end apart: 4, of which 4 were waited for; matrix products, arithmetic and copies ran while one was open for 5% of the time, Pallas kernels for 0%

commit v1 on v0

v1 whole, which is shorter than its diff:
```python
import functools

import jax
import jax.numpy as jnp
from jax import lax
from jax.experimental import pallas as pl
from jax.experimental.pallas import tpu as pltpu
from jax.sharding import PartitionSpec as P

MESH = pl.DeviceIdType.MESH
AXES = ("pipe", "node", "ep")


def flip(index, mask):
    out = index
    bit = 1
    while bit <= mask:
        if mask & bit:
            out = out + bit * (1 - 2 * ((index // bit) % 2))
        bit *= 2
    return out


def relay_kernel(
    sizes,
    parts,
    tokens,
    slots,
    counts,
    scores,
    hidden,
    weight,
    grad_hidden,
    rows_out,
    hidden_out,
    tok_v,
    weight_v,
    send,
    recv,
    mirrored,
    hid,
    total,
    part_send,
    part_recv,
    tok_sem,
    weight_sem,
    send_sem,
    recv_sem,
    fwd_sem,
    mir_sem,
    hsend_sem,
    hrecv_sem,
    hloc_sem,
    psend_sem,
    precv_sem,
):
    n_pipe, n_node, n_ep = sizes
    n_src = n_node * n_ep
    cap, piece = send.shape[2], send.shape[3]
    width = piece * parts
    tok_rows = tok_v.shape[0]
    own_rows = hid.shape[2]
    half = hid.shape[3]
    recv_rows = n_src * cap

    pipe, node, ep = (lax.axis_index(name) for name in AXES)
    mirror = n_pipe - 1 - pipe
    me = node * n_ep + ep
    keep_first = (pipe // (n_pipe // 2)) * half
    give_first = half - keep_first

    tok_loads = {}
    for c in range(parts):
        for e in range(n_ep):
            cols = pl.ds(e * width + c * piece, piece)
            tok_loads[c, e] = pltpu.make_async_copy(
                tokens.at[0, 0, 0, :, cols], tok_v.at[:, cols], tok_sem.at[c, e]
            )
            tok_loads[c, e].start()
    hid_load = pltpu.make_async_copy(
        hidden.at[0, 0, :, pl.ds(pl.multiple_of(keep_first, 128), half)],
        hid.at[0, ep],
        hloc_sem,
    )
    hid_load.start()
    weight_loads = []
    for c in range(parts):
        cols = pl.ds(c * piece, piece)
        load = pltpu.make_async_copy(
            weight.at[0, 0, :, cols], weight_v.at[:, cols], weight_sem.at[c]
        )
        load.start()
        weight_loads.append(load)

    barrier = pltpu.get_barrier_semaphore()
    peers = [
        (pipe, flip(node, k), flip(ep, j))
        for k in range(n_node)
        for j in range(n_ep)
        if k or j
    ] + [(mirror, node, flip(ep, j)) for j in range(n_ep)]
    for peer in peers:
        pl.semaphore_signal(barrier, inc=1, device_id=peer, device_id_type=MESH)

    eye = lax.broadcasted_iota(jnp.int32, (cap, cap), 0) == lax.broadcasted_iota(
        jnp.int32, (cap, cap), 1
    )
    slot_ids = lax.broadcasted_iota(jnp.int32, (cap, 1), 0)
    token_ids = lax.broadcasted_iota(jnp.int32, (cap, tok_rows), 1)
    hot, factor = [], []
    for g in range(n_node):
        slot_row = slots[0, 0, 0, g : g + 1, :]
        score_row = scores[0, 0, 0, g : g + 1, :]
        slot_col = jnp.sum(jnp.where(eye, slot_row, 0), axis=1, keepdims=True)
        score_col = jnp.sum(jnp.where(eye, score_row, 0.0), axis=1, keepdims=True)
        hot.append(jnp.where(token_ids == slot_col, 1.0, 0.0))
        factor.append(jnp.where(slot_ids < counts[0, 0, 0, g], score_col, 0.0))
    hot = jnp.concatenate(hot, axis=0).astype(jnp.bfloat16)
    factor = jnp.concatenate(factor, axis=0)

    def route(c):
        for e in range(n_ep):
            tok_loads[c, e].wait()
            start = e * width + c * piece
            picked = jnp.dot(
                hot, tok_v[:, start : start + piece], preferred_element_type=jnp.float32
            )
            picked = picked * factor
            for g in range(n_node):
                send[c, g * n_ep + e] = picked[g * cap : (g + 1) * cap].astype(jnp.bfloat16)

    sent = []

    def dispatch(c):
        for k in reversed(range(n_node)):
            for j in reversed(range(n_ep)):
                if k == 0 and j == 0:
                    continue
                to_node, to_ep = flip(node, k), flip(ep, j)
                copy = pltpu.make_async_remote_copy(
                    src_ref=send.at[c, to_node * n_ep + to_ep],
                    dst_ref=recv.at[c, me],
                    send_sem=send_sem.at[c, k * n_ep + j],
                    recv_sem=recv_sem.at[c, me],
                    device_id=(pipe, to_node, to_ep),
                    device_id_type=MESH,
                )
                copy.start()
                sent.append(copy)

    def forward(c, source, index, block):
        copy = pltpu.make_async_remote_copy(
            src_ref=block,
            dst_ref=mirrored.at[c, source],
            send_sem=fwd_sem.at[c, index],
            recv_sem=mir_sem.at[c, source],
            device_id=(mirror, node, ep),
            device_id_type=MESH,
        )
        copy.start()
        sent.append(copy)

    route(0)
    pl.semaphore_wait(barrier, len(peers))
    dispatch(0)
    forward(0, me, 0, send.at[0, me])
    for j in range(n_ep):
        copy = pltpu.make_async_remote_copy(
            src_ref=hidden.at[0, 0, :, pl.ds(pl.multiple_of(give_first, 128), half)],
            dst_ref=hid.at[1, ep],
            send_sem=hsend_sem.at[1, j],
            recv_sem=hrecv_sem.at[1, ep],
            device_id=(mirror, node, flip(ep, j)),
            device_id_type=MESH,
        )
        copy.start()
        sent.append(copy)
        if j:
            copy = pltpu.make_async_remote_copy(
                src_ref=hidden.at[0, 0, :, pl.ds(pl.multiple_of(keep_first, 128), half)],
                dst_ref=hid.at[0, ep],
                send_sem=hsend_sem.at[0, j],
                recv_sem=hrecv_sem.at[0, ep],
                device_id=(pipe, node, flip(ep, j)),
                device_id_type=MESH,
            )
            copy.start()
            sent.append(copy)
    for c in range(1, parts):
        route(c)
        dispatch(c)
        forward(c, me, 0, send.at[c, me])
    for c in range(parts):
        recv[c, me] = send[c, me]

    def arrival(buffer, index, sem):
        return pltpu.make_async_remote_copy(
            src_ref=buffer.at[index],
            dst_ref=buffer.at[index],
            send_sem=send_sem.at[0, 0],
            recv_sem=sem.at[index],
            device_id=(mirror, node, ep),
            device_id_type=MESH,
        )

    def gathered(buffer, c):
        blocks = [buffer[c, s].astype(jnp.float32) for s in range(n_src)]
        return jnp.concatenate(blocks, axis=0).astype(jnp.bfloat16)

    for c in range(parts):
        for k in range(n_node):
            for j in range(n_ep):
                if k == 0 and j == 0:
                    continue
                source = flip(node, k) * n_ep + flip(ep, j)
                arrival(recv, (c, source), recv_sem).wait_recv()
                forward(c, source, k * n_ep + j, recv.at[c, source])
        rows = gathered(recv, c)
        rows_out[0:recv_rows, c * piece : (c + 1) * piece] = rows
        weight_loads[c].wait()
        share = lax.dot_general(
            rows,
            weight_v[:, c * piece : (c + 1) * piece],
            (((1,), (1,)), ((), ())),
            preferred_element_type=jnp.float32,
        )
        if c == 0:
            total[...] = share
        else:
            total[...] += share

    for j in range(1, n_ep):
        to_ep = flip(ep, j)
        first = pl.multiple_of(to_ep * own_rows, own_rows)
        part_send[j] = total[pl.ds(first, own_rows), :].astype(jnp.bfloat16)
        copy = pltpu.make_async_remote_copy(
            src_ref=part_send.at[j],
            dst_ref=part_recv.at[ep],
            send_sem=psend_sem.at[j],
            recv_sem=precv_sem.at[ep],
            device_id=(pipe, node, to_ep),
            device_id_type=MESH,
        )
        copy.start()
        sent.append(copy)

    hid_load.wait()
    for j in range(n_ep):
        source = flip(ep, j)
        arrival(hid, (1, source), hrecv_sem).wait_recv()
        if j:
            arrival(hid, (0, source), hrecv_sem).wait_recv()
    for copy_at in range(2):
        for e in range(n_ep):
            first = (copy_at * n_ep + e) * own_rows
            hidden_out[first : first + own_rows, :] = hid[copy_at, e]

    for c in range(parts):
        for k in range(n_node):
            for j in range(n_ep):
                source = flip(node, k) * n_ep + flip(ep, j)
                arrival(mirrored, (c, source), mir_sem).wait_recv()
        rows_out[recv_rows:, c * piece : (c + 1) * piece] = gathered(mirrored, c)

    first = pl.multiple_of(ep * own_rows, own_rows)
    own = total[pl.ds(first, own_rows), :]
    for j in range(1, n_ep):
        source = flip(ep, j)
        arrival(part_recv, (source,), precv_sem).wait_recv()
        own = own + part_recv[source].astype(jnp.float32)
    grad_hidden[0, 0] = own.astype(jnp.bfloat16)
    for copy in sent:
        copy.wait_send()


def weight_kernel(hidden, rows, out):
    out[0, 0] = lax.dot_general(
        hidden[...], rows[...], (((0,), (0,)), ((), ())), preferred_element_type=jnp.float32
    ).astype(jnp.bfloat16)


def local(sizes, grad_tokens, slot_token, send_count, route_score, hidden_act, w_down):
    n_pipe, n_node, n_ep = sizes
    n_src = n_node * n_ep
    tok_rows, features = grad_tokens.shape[-2:]
    cap = slot_token.shape[-1]
    own_rows, units = hidden_act.shape[-2:]
    width = w_down.shape[-1]
    half = units // 2
    recv_rows = n_src * cap
    parts = 2 if (width // 128) % 2 == 0 else 1
    piece = width // parts
    bf16, f32 = jnp.bfloat16, jnp.float32
    dma = pltpu.SemaphoreType.DMA
    vmem = pl.BlockSpec(memory_space=pltpu.VMEM)
    hbm = pl.BlockSpec(memory_space=pl.ANY)
    grad_hidden, rows, hidden = pl.pallas_call(
        functools.partial(relay_kernel, sizes, parts),
        out_shape=(
            jax.ShapeDtypeStruct((1, 1, own_rows, units), bf16),
            jax.ShapeDtypeStruct((2 * recv_rows, width), bf16),
            jax.ShapeDtypeStruct((2 * recv_rows, half), bf16),
        ),
        in_specs=[hbm, vmem, pl.BlockSpec(memory_space=pltpu.SMEM), vmem, hbm, hbm],
        out_specs=(vmem, vmem, vmem),
        scratch_shapes=[
            pltpu.VMEM((tok_rows, features), bf16),
            pltpu.VMEM((units, width), bf16),
            pltpu.VMEM((parts, n_src, cap, piece), bf16),
            pltpu.VMEM((parts, n_src, cap, piece), bf16),
            pltpu.VMEM((parts, n_src, cap, piece), bf16),
            pltpu.VMEM((2, n_ep, own_rows, half), bf16),
            pltpu.VMEM((recv_rows, units), f32),
            pltpu.VMEM((n_ep, own_rows, units), bf16),
            pltpu.VMEM((n_ep, own_rows, units), bf16),
            dma((parts, n_ep)),
            dma((parts,)),
            dma((parts, n_src)),
            dma((parts, n_src)),
            dma((parts, n_src)),
            dma((parts, n_src)),
            dma((2, n_ep)),
            dma((2, n_ep)),
            dma,
            dma((n_ep,)),
            dma((n_ep,)),
        ],
        compiler_params=pltpu.CompilerParams(
            collective_id=0, has_side_effects=True, vmem_limit_bytes=40 * 2**20
        ),
    )(grad_tokens, slot_token, send_count, route_score, hidden_act, w_down)

    tile = 512 if width % 512 == 0 else 128
    grad_weight = pl.pallas_call(
        weight_kernel,
        grid=(width // tile,),
        out_shape=jax.ShapeDtypeStruct((1, 1, half, width), bf16),
        in_specs=[
            pl.BlockSpec((2 * recv_rows, half), lambda i: (0, 0)),
            pl.BlockSpec((2 * recv_rows, tile), lambda i: (0, i)),
        ],
        out_specs=pl.BlockSpec((1, 1, half, tile), lambda i: (0, 0, 0, i)),
        compiler_params=pltpu.CompilerParams(vmem_limit_bytes=24 * 2**20),
    )(hidden, rows)
    return grad_hidden, grad_weight


def solution(mesh):
    sizes = tuple(mesh.shape[name] for name in AXES)
    in_specs = (
        P("pipe", "node", "ep", None, None),
        P("pipe", "node", "ep", None, None),
        P("pipe", "node", "ep", None),
        P("pipe", "node", "ep", None, None),
        P("pipe", "node", "ep", None),
        P("pipe", "node", None, "ep"),
    )
    out_specs = (P("pipe", "node", "ep", None), P("pipe", "node", None, "ep"))
    return jax.shard_map(
        functools.partial(local, sizes),
        mesh=mesh,
        in_specs=in_specs,
        out_specs=out_specs,
        check_vma=False,
    )
```

time: 147 us -> 37.6 us (0.26)
  waiting for transfers between devices: 84.9 us -> 0 us
  Pallas kernels: 0 us -> 28.6 us
  between operations: 14.1 us -> 0.65 us
  other arithmetic: 10 us -> 0 us
  starting transfers between devices: 8.88 us -> 0 us
  matrix products: 8.19 us -> 0 us
  blocking collectives: 7.14 us -> 0 us
  local copies, waits for them, and re-layouts: 12.9 us -> 8.06 us
    ppermute x2 -> x0, waiting for transfers between devices: 69.1 us -> none  [partner(): return lax.ppermute(value, axis, pairs)]
    pallas_call x0 -> x2, Pallas kernels: none -> 28.6 us  [the longest x1 24 us: local(): pl.pallas_call(functools.partial(relay_kernel, sizes, parts), out_shape=(...]
    reduce_scatter x1 -> x0, waiting for transfers between devices: 9.93 us -> none  [local(): lax.psum_scatter(lax.dot_general(row_block, weight_slice, (((1,), (1,)),...]
    dot_general x2 -> x0, matrix products: 8.19 us -> none  [the longest x1 6.1 us: local(): lax.dot_general(row_block, weight_slice, (((1,), (1,)), ((), ())), prefer...]
    broadcast_in_dim x2 -> x0, other arithmetic: 7.64 us -> none  [local(): return (grad_hidden[None, None], grad_weight[None, None])]
    all_to_all x1 -> x0, starting transfers between devices: 7.25 us -> none  [local(): lax.all_to_all(routed.reshape(groups * owners, capacity, slice_width), ('...]
    all_gather x1 -> x0, blocking collectives: 7.14 us -> none  [local(): lax.all_gather(own_hidden, 'ep', axis=0, tiled=True)]
    all_to_all x1 -> x0, waiting for transfers between devices: 5.87 us -> none  [local(): lax.all_to_all(routed.reshape(groups * owners, capacity, slice_width), ('...]
  transfers between devices with their start and end apart: 4 -> 0, of which waited for: 4 -> 0; matrix products, arithmetic and copies ran while one was open for 5% -> 0% of each run, Pallas kernels for 0% -> 0%
where the time goes in v1:
time: 37.6 us; the launch traced here: 37.3 us
  Pallas kernels  28.6 us (76%)
  local copies, waits for them, and re-layouts  8.06 us (21%)
  between operations  0.65 us (2%)
    pallas_call x1, Pallas kernels, local(): pl.pallas_call(functools.partial(relay_kernel, sizes, parts), out_shape=(...  24 us
    unnamed x13, local copies, waits for them, and re-layouts  8.06 us
    pallas_call x1, Pallas kernels, local(): pl.pallas_call(weight_kernel, grid=(width // tile,), out_shape=jax.ShapeD...  4.51 us

profile of v1, /device:TPU:0, one launch (start us, length us, event | category | flops | bytes accessed | tf_op | source)
XLA Modules:
  0.0 37.3 jit_solution(17230298332286262874)
XLA Ops:
  0.6 0.0 copy-start
  0.6 3.1 %copy-done = bf16[1,1,1024,3584]{3,2,1,0:T(8,128)(2,1)S(1)} copy-done((bf16[1,1,1024,3584]{3,2,1,0:T(8,128)(2,1)S(1)}, bf16[1,1,1024,3584]{3,2,1,0:T(8,128)(2,1)}, u32[]{:S(2)}) %copy-start) | copy-done | bytes 7340056
  3.7 0.0 copy-start.1
  3.7 1.5 %copy-done.1 = bf16[1,1,1,128,7168]{4,3,2,1,0:T(8,128)(2,1)S(1)} copy-done((bf16[1,1,1,128,7168]{4,3,2,1,0:T(8,128)(2,1)S(1)}, bf16[1,1,1,128,7168]{4,3,2,1,0:T(8,128)(2,1)}, u32[]{:S(2)}) %copy-start.1) | copy-done | bytes 1835032
  5.2 0.0 copy-start.2
  5.2 0.8 %copy-done.2 = bf16[1,1,32,1024]{3,2,1,0:T(8,128)(2,1)S(1)} copy-done((bf16[1,1,32,1024]{3,2,1,0:T(8,128)(2,1)S(1)}, bf16[1,1,32,1024]{3,2,1,0:T(8,128)(2,1)}, u32[]{:S(2)}) %copy-start.2) | copy-done | bytes 65560
  6.1 0.0 copy-start.3
  6.1 0.7 %copy-done.3 = s32[1,1,1,4,8]{4,3,2,1,0:T(4,128)S(1)} copy-done((s32[1,1,1,4,8]{4,3,2,1,0:T(4,128)S(1)}, s32[1,1,1,4,8]{4,3,2,1,0:T(4,128)}, u32[]{:S(2)}) %copy-start.3) | copy-done | bytes 152
  6.7 0.0 copy-start.4
  6.7 0.7 %copy-done.4 = f32[1,1,1,4,8]{4,3,2,1,0:T(4,128)S(1)} copy-done((f32[1,1,1,4,8]{4,3,2,1,0:T(4,128)S(1)}, f32[1,1,1,4,8]{4,3,2,1,0:T(4,128)}, u32[]{:S(2)}) %copy-start.4) | copy-done | bytes 152
  7.4 0.0 copy-start.5
  7.4 0.7 %copy-done.5 = s32[1,1,1,4]{3,2,1,0:T(1,128)S(1)} copy-done((s32[1,1,1,4]{3,2,1,0:T(1,128)S(1)}, s32[1,1,1,4]{3,2,1,0:T(1,128)}, u32[]{:S(2)}) %copy-start.5) | copy-done | bytes 40
  8.1 24.0 %shard_map.77 = (bf16[1,1,32,1024]{3,2,1,0:T(8,128)(2,1)S(1)}, bf16[128,3584]{1,0:T(8,128)(2,1)S(1)}, bf16[128,512]{1,0:T(8,128)(2,1)S(1)}) custom-call(bf16[1,1,1,128,7168]{4,3,2,1,0:T(8,128)(2,1)S(1)} %copy-done.1, s32[1,1,1,4,8]{4,3,2,1,0:T(4,128)S(1)} %copy-done.3, s32[1,1,1,4]{3,2,1,0:T(1,128)S(1)} %copy-done.5, f32[1,1,1,4,8]{4,3,2,1,0:T(4,128)S(1)} %copy-done.4, ...), custom_call_target="tpu_custom_call" | custom-call | tf_op jit(solution)/shard_map/pallas_call | solution.py:297
  32.1 4.5 %shard_map.78 = bf16[1,1,512,3584]{3,2,1,0:T(8,128)(2,1)} custom-call(bf16[128,512]{1,0:T(8,128)(2,1)S(1)} %get-tuple-element.6.hidden, bf16[128,3584]{1,0:T(8,128)(2,1)S(1)} %get-tuple-element.7.rows), custom_call_target="tpu_custom_call" | custom-call | tf_op jit(solution)/shard_map/pallas_call | solution.py:334
  36.6 0.6 %copy.9 = bf16[1,1,32,1024]{3,2,1,0:T(8,128)(2,1)} copy(bf16[1,1,32,1024]{3,2,1,0:T(8,128)(2,1)S(1)} %get-tuple-element.10) | data formatting | bytes 131072
Async XLA Ops:
  0.6 3.1 %copy-start = (bf16[1,1,1024,3584]{3,2,1,0:T(8,128)(2,1)S(1)}, bf16[1,1,1024,3584]{3,2,1,0:T(8,128)(2,1)}, u32[]{:S(2)}) copy-start(bf16[1,1,1024,3584]{3,2,1,0:T(8,128)(2,1)} %weight.1) | copy-start | bytes 22020100
  3.7 1.5 %copy-start.1 = (bf16[1,1,1,128,7168]{4,3,2,1,0:T(8,128)(2,1)S(1)}, bf16[1,1,1,128,7168]{4,3,2,1,0:T(8,128)(2,1)}, u32[]{:S(2)}) copy-start(bf16[1,1,1,128,7168]{4,3,2,1,0:T(8,128)(2,1)} %tokens.1) | copy-start | bytes 5505028
  5.2 0.8 %copy-start.2 = (bf16[1,1,32,1024]{3,2,1,0:T(8,128)(2,1)S(1)}, bf16[1,1,32,1024]{3,2,1,0:T(8,128)(2,1)}, u32[]{:S(2)}) copy-start(bf16[1,1,32,1024]{3,2,1,0:T(8,128)(2,1)} %hidden.1) | copy-start | bytes 196612
  6.1 0.7 %copy-start.3 = (s32[1,1,1,4,8]{4,3,2,1,0:T(4,128)S(1)}, s32[1,1,1,4,8]{4,3,2,1,0:T(4,128)}, u32[]{:S(2)}) copy-start(s32[1,1,1,4,8]{4,3,2,1,0:T(4,128)} %slots.1) | copy-start | bytes 388
  6.7 0.7 %copy-start.4 = (f32[1,1,1,4,8]{4,3,2,1,0:T(4,128)S(1)}, f32[1,1,1,4,8]{4,3,2,1,0:T(4,128)}, u32[]{:S(2)}) copy-start(f32[1,1,1,4,8]{4,3,2,1,0:T(4,128)} %scores.1) | copy-start | bytes 388
  7.4 0.7 %copy-start.5 = (s32[1,1,1,4]{3,2,1,0:T(1,128)S(1)}, s32[1,1,1,4]{3,2,1,0:T(1,128)}, u32[]{:S(2)}) copy-start(s32[1,1,1,4]{3,2,1,0:T(1,128)} %counts.1) | copy-start | bytes 52

commit v2 on v1

--- a/solution.py
+++ b/solution.py
@@ -33,15 +33,22 @@
     grad_hidden,
     rows_out,
     hidden_out,
+    slots_v,
+    counts_v,
+    scores_v,
     tok_v,
     weight_v,
     send,
     recv,
     mirrored,
     hid,
+    hid_all,
+    hid_turned,
+    rows_all,
     total,
     part_send,
     part_recv,
+    small_sem,
     tok_sem,
     weight_sem,
     send_sem,
@@ -51,6 +58,8 @@
     hsend_sem,
     hrecv_sem,
     hloc_sem,
+    rows_sem,
+    turned_sem,
     psend_sem,
     precv_sem,
 ):
@@ -69,6 +78,13 @@
     keep_first = (pipe // (n_pipe // 2)) * half
     give_first = half - keep_first
 
+    small_loads = [
+        pltpu.make_async_copy(slots.at[0, 0, 0], slots_v, small_sem.at[0]),
+        pltpu.make_async_copy(counts.at[0, 0], counts_v, small_sem.at[1]),
+        pltpu.make_async_copy(scores.at[0, 0, 0], scores_v, small_sem.at[2]),
+    ]
+    for load in small_loads:
+        load.start()
     tok_loads = {}
     for c in range(parts):
         for e in range(n_ep):
@@ -108,13 +124,15 @@
     slot_ids = lax.broadcasted_iota(jnp.int32, (cap, 1), 0)
     token_ids = lax.broadcasted_iota(jnp.int32, (cap, tok_rows), 1)
     hot, factor = [], []
+    for load in small_loads:
+        load.wait()
     for g in range(n_node):
-        slot_row = slots[0, 0, 0, g : g + 1, :]
-        score_row = scores[0, 0, 0, g : g + 1, :]
+        slot_row = slots_v[g : g + 1, :]
+        score_row = scores_v[g : g + 1, :]
         slot_col = jnp.sum(jnp.where(eye, slot_row, 0), axis=1, keepdims=True)
         score_col = jnp.sum(jnp.where(eye, score_row, 0.0), axis=1, keepdims=True)
         hot.append(jnp.where(token_ids == slot_col, 1.0, 0.0))
-        factor.append(jnp.where(slot_ids < counts[0, 0, 0, g], score_col, 0.0))
+        factor.append(jnp.where(slot_ids < counts_v[0, g], score_col, 0.0))
     hot = jnp.concatenate(hot, axis=0).astype(jnp.bfloat16)
     factor = jnp.concatenate(factor, axis=0)
 
@@ -129,10 +147,19 @@
             for g in range(n_node):
                 send[c, g * n_ep + e] = picked[g * cap : (g + 1) * cap].astype(jnp.bfloat16)
 
-    sent = []
+    sent, stores = [], []
+
+    def store_rows(c, at, value):
+        block = (pl.ds(at * recv_rows, recv_rows), pl.ds(c * piece, piece))
+        rows_all[block] = value
+        store = pltpu.make_async_copy(
+            rows_all.at[block], rows_out.at[block], rows_sem.at[at, c]
+        )
+        store.start()
+        stores.append(store)
 
     def dispatch(c):
-        for k in reversed(range(n_node)):
+        for k in range(n_node):
             for j in reversed(range(n_ep)):
                 if k == 0 and j == 0:
                     continue
@@ -207,6 +234,21 @@
         blocks = [buffer[c, s].astype(jnp.float32) for s in range(n_src)]
         return jnp.concatenate(blocks, axis=0).astype(jnp.bfloat16)
 
+    hid_load.wait()
+    for j in range(n_ep):
+        source = flip(ep, j)
+        arrival(hid, (1, source), hrecv_sem).wait_recv()
+        if j:
+            arrival(hid, (0, source), hrecv_sem).wait_recv()
+    for copy_at in range(2):
+        for e in range(n_ep):
+            first = (copy_at * n_ep + e) * own_rows
+            hid_all[first : first + own_rows, :] = hid[copy_at, e].astype(jnp.float32)
+    hid_turned[...] = hid_all[...].T.astype(jnp.bfloat16)
+    store = pltpu.make_async_copy(hid_turned, hidden_out, turned_sem)
+    store.start()
+    stores.append(store)
+
     for c in range(parts):
         for k in range(n_node):
             for j in range(n_ep):
@@ -216,7 +258,7 @@
                 arrival(recv, (c, source), recv_sem).wait_recv()
                 forward(c, source, k * n_ep + j, recv.at[c, source])
         rows = gathered(recv, c)
-        rows_out[0:recv_rows, c * piece : (c + 1) * piece] = rows
+        store_rows(c, 0, rows)
         weight_loads[c].wait()
         share = lax.dot_general(
             rows,
@@ -244,23 +286,12 @@
         copy.start()
         sent.append(copy)
 
-    hid_load.wait()
-    for j in range(n_ep):
-        source = flip(ep, j)
-        arrival(hid, (1, source), hrecv_sem).wait_recv()
-        if j:
-            arrival(hid, (0, source), hrecv_sem).wait_recv()
-    for copy_at in range(2):
-        for e in range(n_ep):
-            first = (copy_at * n_ep + e) * own_rows
-            hidden_out[first : first + own_rows, :] = hid[copy_at, e]
-
     for c in range(parts):
         for k in range(n_node):
             for j in range(n_ep):
                 source = flip(node, k) * n_ep + flip(ep, j)
                 arrival(mirrored, (c, source), mir_sem).wait_recv()
-        rows_out[recv_rows:, c * piece : (c + 1) * piece] = gathered(mirrored, c)
+        store_rows(c, 1, gathered(mirrored, c))
 
     first = pl.multiple_of(ep * own_rows, own_rows)
     own = total[pl.ds(first, own_rows), :]
@@ -271,12 +302,34 @@
     grad_hidden[0, 0] = own.astype(jnp.bfloat16)
     for copy in sent:
         copy.wait_send()
-
-
-def weight_kernel(hidden, rows, out):
-    out[0, 0] = lax.dot_general(
-        hidden[...], rows[...], (((0,), (0,)), ((), ())), preferred_element_type=jnp.float32
-    ).astype(jnp.bfloat16)
+    for store in stores:
+        store.wait()
+
+
+def weight_kernel(hidden, rows, out, hid_v, rows_v, out_v, load_sem, store_sem):
+    loads = [
+        pltpu.make_async_copy(hidden, hid_v, load_sem.at[0]),
+        pltpu.make_async_copy(rows, rows_v, load_sem.at[1]),
+    ]
+    for load in loads:
+        load.start()
+    for load in loads:
+        load.wait()
+    steps = store_sem.shape[0]
+    tall = hid_v.shape[0] // steps
+    stores = []
+    for m in range(steps):
+        block = pl.ds(m * tall, tall)
+        out_v[block, :] = jnp.dot(
+            hid_v[block, :], rows_v[...], preferred_element_type=jnp.float32
+        ).astype(jnp.bfloat16)
+        store = pltpu.make_async_copy(
+            out_v.at[block, :], out.at[0, 0, block, :], store_sem.at[m]
+        )
+        store.start()
+        stores.append(store)
+    for store in stores:
+        store.wait()
 
 
 def local(sizes, grad_tokens, slot_token, send_count, route_score, hidden_act, w_down):
@@ -293,26 +346,33 @@
     bf16, f32 = jnp.bfloat16, jnp.float32
     dma = pltpu.SemaphoreType.DMA
     vmem = pl.BlockSpec(memory_space=pltpu.VMEM)
-    hbm = pl.BlockSpec(memory_space=pl.ANY)
+    hbm = pl.BlockSpec(memory_space=pltpu.HBM)
     grad_hidden, rows, hidden = pl.pallas_call(
         functools.partial(relay_kernel, sizes, parts),
         out_shape=(
             jax.ShapeDtypeStruct((1, 1, own_rows, units), bf16),
             jax.ShapeDtypeStruct((2 * recv_rows, width), bf16),
-            jax.ShapeDtypeStruct((2 * recv_rows, half), bf16),
+            jax.ShapeDtypeStruct((half, 2 * recv_rows), bf16),
         ),
-        in_specs=[hbm, vmem, pl.BlockSpec(memory_space=pltpu.SMEM), vmem, hbm, hbm],
-        out_specs=(vmem, vmem, vmem),
+        in_specs=[hbm] * 6,
+        out_specs=(vmem, hbm, hbm),
         scratch_shapes=[
+            pltpu.VMEM((n_node, cap), jnp.int32),
+            pltpu.SMEM((1, n_node), jnp.int32),
+            pltpu.VMEM((n_node, cap), f32),
             pltpu.VMEM((tok_rows, features), bf16),
             pltpu.VMEM((units, width), bf16),
             pltpu.VMEM((parts, n_src, cap, piece), bf16),
             pltpu.VMEM((parts, n_src, cap, piece), bf16),
             pltpu.VMEM((parts, n_src, cap, piece), bf16),
             pltpu.VMEM((2, n_ep, own_rows, half), bf16),
+            pltpu.VMEM((2 * recv_rows, half), f32),
+            pltpu.VMEM((half, 2 * recv_rows), bf16),
+            pltpu.VMEM((2 * recv_rows, width), bf16),
             pltpu.VMEM((recv_rows, units), f32),
             pltpu.VMEM((n_ep, own_rows, units), bf16),
             pltpu.VMEM((n_ep, own_rows, units), bf16),
+            dma((3,)),
             dma((parts, n_ep)),
             dma((parts,)),
             dma((parts, n_src)),
@@ -322,25 +382,30 @@
             dma((2, n_ep)),
             dma((2, n_ep)),
             dma,
+            dma((2, parts)),
+            dma,
             dma((n_ep,)),
             dma((n_ep,)),
         ],
         compiler_params=pltpu.CompilerParams(
-            collective_id=0, has_side_effects=True, vmem_limit_bytes=40 * 2**20
+            collective_id=0, has_side_effects=True, vmem_limit_bytes=63 * 2**20
         ),
     )(grad_tokens, slot_token, send_count, route_score, hidden_act, w_down)
 
-    tile = 512 if width % 512 == 0 else 128
+    steps = 4
     grad_weight = pl.pallas_call(
         weight_kernel,
-        grid=(width // tile,),
         out_shape=jax.ShapeDtypeStruct((1, 1, half, width), bf16),
-        in_specs=[
-            pl.BlockSpec((2 * recv_rows, half), lambda i: (0, 0)),
-            pl.BlockSpec((2 * recv_rows, tile), lambda i: (0, i)),
+        in_specs=[hbm, hbm],
+        out_specs=hbm,
+        scratch_shapes=[
+            pltpu.VMEM((half, 2 * recv_rows), bf16),
+            pltpu.VMEM((2 * recv_rows, width), bf16),
+            pltpu.VMEM((half, width), bf16),
+            dma((2,)),
+            dma((steps,)),
         ],
-        out_specs=pl.BlockSpec((1, 1, half, tile), lambda i: (0, 0, 0, i)),
-        compiler_params=pltpu.CompilerParams(vmem_limit_bytes=24 * 2**20),
+        compiler_params=pltpu.CompilerParams(vmem_limit_bytes=63 * 2**20),
     )(hidden, rows)
     return grad_hidden, grad_weight
 

time: 37.6 us -> 28.6 us (0.76)
  local copies, waits for them, and re-layouts: 8.06 us -> 0.64 us
  Pallas kernels: 28.6 us -> 26.7 us
    unnamed x13 -> x3, local copies, waits for them, and re-layouts: 8.06 us -> 0.64 us
    pallas_call x1, Pallas kernels: 4.51 us -> 3.54 us  [local(): pl.pallas_call(weight_kernel, out_shape=jax.ShapeDtypeStruct((1, 1, half,...]
    pallas_call x1, Pallas kernels: 24 us -> 23.2 us  [local(): pl.pallas_call(functools.partial(relay_kernel, sizes, parts), out_shape=(...]
where the time goes in v2:
time: 28.6 us; the launch traced here: 28 us
  Pallas kernels  26.7 us (93%)
  between operations  0.66 us (2%)
  local copies, waits for them, and re-layouts  0.64 us (2%)
    pallas_call x1, Pallas kernels, local(): pl.pallas_call(functools.partial(relay_kernel, sizes, parts), out_shape=(...  23.2 us
    pallas_call x1, Pallas kernels, local(): pl.pallas_call(weight_kernel, out_shape=jax.ShapeDtypeStruct((1, 1, half,...  3.54 us
    unnamed x3, local copies, waits for them, and re-layouts  0.64 us

profile of v2, /device:TPU:0, one launch (start us, length us, event | category | flops | bytes accessed | tf_op | source)
XLA Modules:
  0.0 28.0 jit_solution(9332086658356722141)
XLA Ops:
  0.6 23.2 %shard_map.77 = (bf16[1,1,32,1024]{3,2,1,0:T(8,128)(2,1)}, bf16[128,3584]{1,0:T(8,128)(2,1)}, bf16[512,128]{1,0:T(8,128)(2,1)}) custom-call(bf16[1,1,1,128,7168]{4,3,2,1,0:T(8,128)(2,1)} %tokens.1, s32[1,1,1,4,8]{4,3,2,1,0:T(4,128)} %slots.1, s32[1,1,1,4]{3,2,1,0:T(1,128)} %counts.1, f32[1,1,1,4,8]{4,3,2,1,0:T(4,128)} %scores.1, ...), custom_call_target="tpu_custom_call" | custom-call | tf_op jit(solution)/shard_map/pallas_call | solution.py:350
  23.8 0.0 copy-start
  23.8 3.5 %shard_map.78 = bf16[1,1,512,3584]{3,2,1,0:T(8,128)(2,1)} custom-call(bf16[512,128]{1,0:T(8,128)(2,1)} %get-tuple-element.6.hidden, bf16[128,3584]{1,0:T(8,128)(2,1)} %get-tuple-element.7.rows), custom_call_target="tpu_custom_call" | custom-call | tf_op jit(solution)/shard_map/pallas_call | solution.py:396
  27.4 0.0 copy-done
  27.4 0.6 %copy.9 = bf16[1,1,32,1024]{3,2,1,0:T(8,128)(2,1)} copy(bf16[1,1,32,1024]{3,2,1,0:T(8,128)(2,1)S(1)} %copy-done) | data formatting | bytes 131072
Async XLA Ops:
  23.8 3.6 %copy-start = (bf16[1,1,32,1024]{3,2,1,0:T(8,128)(2,1)S(1)}, bf16[1,1,32,1024]{3,2,1,0:T(8,128)(2,1)}, u32[]{:S(2)}) copy-start(bf16[1,1,32,1024]{3,2,1,0:T(8,128)(2,1)} %get-tuple-element.10) | copy-start | bytes 196612

commit v3 on v2

--- a/solution.py
+++ b/solution.py
@@ -30,9 +30,9 @@
     scores,
     hidden,
     weight,
-    grad_hidden,
     rows_out,
     hidden_out,
+    shares_out,
     slots_v,
     counts_v,
     scores_v,
@@ -60,6 +60,7 @@
     hloc_sem,
     rows_sem,
     turned_sem,
+    shares_sem,
     psend_sem,
     precv_sem,
 ):
@@ -160,7 +161,7 @@
 
     def dispatch(c):
         for k in range(n_node):
-            for j in reversed(range(n_ep)):
+            for j in range(n_ep):
                 if k == 0 and j == 0:
                     continue
                 to_node, to_ep = flip(node, k), flip(ep, j)
@@ -271,6 +272,11 @@
         else:
             total[...] += share
 
+    first = pl.multiple_of(ep * own_rows, own_rows)
+    part_send[0] = total[pl.ds(first, own_rows), :].astype(jnp.bfloat16)
+    store = pltpu.make_async_copy(part_send.at[0], shares_out.at[ep], shares_sem.at[0])
+    store.start()
+    stores.append(store)
     for j in range(1, n_ep):
         to_ep = flip(ep, j)
         first = pl.multiple_of(to_ep * own_rows, own_rows)
@@ -293,27 +299,43 @@
                 arrival(mirrored, (c, source), mir_sem).wait_recv()
         store_rows(c, 1, gathered(mirrored, c))
 
-    first = pl.multiple_of(ep * own_rows, own_rows)
-    own = total[pl.ds(first, own_rows), :]
     for j in range(1, n_ep):
         source = flip(ep, j)
         arrival(part_recv, (source,), precv_sem).wait_recv()
-        own = own + part_recv[source].astype(jnp.float32)
-    grad_hidden[0, 0] = own.astype(jnp.bfloat16)
+        store = pltpu.make_async_copy(
+            part_recv.at[source], shares_out.at[source], shares_sem.at[j]
+        )
+        store.start()
+        stores.append(store)
     for copy in sent:
         copy.wait_send()
     for store in stores:
         store.wait()
 
 
-def weight_kernel(hidden, rows, out, hid_v, rows_v, out_v, load_sem, store_sem):
+def weight_kernel(
+    hidden,
+    rows,
+    shares,
+    grad_hidden,
+    grad_weight,
+    hid_v,
+    rows_v,
+    shares_v,
+    small_v,
+    out_v,
+    load_sem,
+    small_sem,
+    store_sem,
+):
     loads = [
         pltpu.make_async_copy(hidden, hid_v, load_sem.at[0]),
         pltpu.make_async_copy(rows, rows_v, load_sem.at[1]),
+        pltpu.make_async_copy(shares, shares_v, load_sem.at[2]),
     ]
     for load in loads:
         load.start()
-    for load in loads:
+    for load in loads[:2]:
         load.wait()
     steps = store_sem.shape[0]
     tall = hid_v.shape[0] // steps
@@ -324,10 +346,19 @@
             hid_v[block, :], rows_v[...], preferred_element_type=jnp.float32
         ).astype(jnp.bfloat16)
         store = pltpu.make_async_copy(
-            out_v.at[block, :], out.at[0, 0, block, :], store_sem.at[m]
+            out_v.at[block, :], grad_weight.at[0, 0, block, :], store_sem.at[m]
         )
         store.start()
         stores.append(store)
+        if m == 0:
+            loads[2].wait()
+            summed = shares_v[0].astype(jnp.float32)
+            for e in range(1, shares_v.shape[0]):
+                summed = summed + shares_v[e].astype(jnp.float32)
+            small_v[...] = summed.astype(jnp.bfloat16)
+            store = pltpu.make_async_copy(small_v, grad_hidden.at[0, 0], small_sem)
+            store.start()
+            stores.append(store)
     for store in stores:
         store.wait()
 
@@ -345,17 +376,16 @@
     piece = width // parts
     bf16, f32 = jnp.bfloat16, jnp.float32
     dma = pltpu.SemaphoreType.DMA
-    vmem = pl.BlockSpec(memory_space=pltpu.VMEM)
     hbm = pl.BlockSpec(memory_space=pltpu.HBM)
-    grad_hidden, rows, hidden = pl.pallas_call(
+    rows, hidden, shares = pl.pallas_call(
         functools.partial(relay_kernel, sizes, parts),
         out_shape=(
-            jax.ShapeDtypeStruct((1, 1, own_rows, units), bf16),
             jax.ShapeDtypeStruct((2 * recv_rows, width), bf16),
             jax.ShapeDtypeStruct((half, 2 * recv_rows), bf16),
+            jax.ShapeDtypeStruct((n_ep, own_rows, units), bf16),
         ),
         in_specs=[hbm] * 6,
-        out_specs=(vmem, hbm, hbm),
+        out_specs=(hbm, hbm, hbm),
         scratch_shapes=[
             pltpu.VMEM((n_node, cap), jnp.int32),
             pltpu.SMEM((1, n_node), jnp.int32),
@@ -386,28 +416,34 @@
             dma,
             dma((n_ep,)),
             dma((n_ep,)),
+            dma((n_ep,)),
         ],
         compiler_params=pltpu.CompilerParams(
             collective_id=0, has_side_effects=True, vmem_limit_bytes=63 * 2**20
         ),
     )(grad_tokens, slot_token, send_count, route_score, hidden_act, w_down)
 
-    steps = 4
-    grad_weight = pl.pallas_call(
+    steps = 8
+    return pl.pallas_call(
         weight_kernel,
-        out_shape=jax.ShapeDtypeStruct((1, 1, half, width), bf16),
-        in_specs=[hbm, hbm],
-        out_specs=hbm,
+        out_shape=(
+            jax.ShapeDtypeStruct((1, 1, own_rows, units), bf16),
+            jax.ShapeDtypeStruct((1, 1, half, width), bf16),
+        ),
+        in_specs=[hbm, hbm, hbm],
+        out_specs=(hbm, hbm),
         scratch_shapes=[
             pltpu.VMEM((half, 2 * recv_rows), bf16),
             pltpu.VMEM((2 * recv_rows, width), bf16),
+            pltpu.VMEM((n_ep, own_rows, units), bf16),
+            pltpu.VMEM((own_rows, units), bf16),
             pltpu.VMEM((half, width), bf16),
-            dma((2,)),
+            dma((3,)),
+            dma,
             dma((steps,)),
         ],
         compiler_params=pltpu.CompilerParams(vmem_limit_bytes=63 * 2**20),
-    )(hidden, rows)
-    return grad_hidden, grad_weight
+    )(hidden, rows, shares)
 
 
 def solution(mesh):

time: 28.6 us -> 27.6 us (0.965); the launches traced: 28 us -> 27.5 us
  local copies, waits for them, and re-layouts: 0.64 us -> 0 us
    unnamed x3 -> x0, local copies, waits for them, and re-layouts: 0.64 us -> none
where the time goes in v3:
time: 27.6 us; the launch traced here: 27.5 us
  Pallas kernels  26.8 us (97%)
  between operations  0.64 us (2%)
    pallas_call x1, Pallas kernels, local(): pl.pallas_call(functools.partial(relay_kernel, sizes, parts), out_shape=(...  23.2 us
    pallas_call x1, Pallas kernels, local(): pl.pallas_call(weight_kernel, out_shape=(jax.ShapeDtypeStruct((1, 1, own_...  3.61 us

profile of v3, /device:TPU:0, one launch (start us, length us, event | category | flops | bytes accessed | tf_op | source)
XLA Modules:
  0.0 27.5 jit_solution(13095406524320308271)
XLA Ops:
  0.6 23.2 %shard_map.77 = (bf16[128,3584]{1,0:T(8,128)(2,1)}, bf16[512,128]{1,0:T(8,128)(2,1)}, bf16[2,32,1024]{2,1,0:T(8,128)(2,1)}) custom-call(bf16[1,1,1,128,7168]{4,3,2,1,0:T(8,128)(2,1)} %tokens.1, s32[1,1,1,4,8]{4,3,2,1,0:T(4,128)} %slots.1, s32[1,1,1,4]{3,2,1,0:T(1,128)} %counts.1, f32[1,1,1,4,8]{4,3,2,1,0:T(4,128)} %scores.1, ...), custom_call_target="tpu_custom_call" | custom-call | tf_op jit(solution)/shard_map/pallas_call | solution.py:380
  23.9 3.6 %shard_map.78 = (bf16[1,1,32,1024]{3,2,1,0:T(8,128)(2,1)}, bf16[1,1,512,3584]{3,2,1,0:T(8,128)(2,1)}) custom-call(bf16[512,128]{1,0:T(8,128)(2,1)} %get-tuple-element.5.hidden, bf16[128,3584]{1,0:T(8,128)(2,1)} %get-tuple-element.6.rows, bf16[2,32,1024]{2,1,0:T(8,128)(2,1)} %get-tuple-element.7.shares), custom_call_target="tpu_custom_call" | custom-call | tf_op jit(solution)/shard_map/pallas_call | solution.py:427

commit v4 on v3

--- a/solution.py
+++ b/solution.py
@@ -330,35 +330,42 @@
 ):
     loads = [
         pltpu.make_async_copy(hidden, hid_v, load_sem.at[0]),
-        pltpu.make_async_copy(rows, rows_v, load_sem.at[1]),
-        pltpu.make_async_copy(shares, shares_v, load_sem.at[2]),
+        pltpu.make_async_copy(shares, shares_v, load_sem.at[1]),
     ]
+    pieces, steps = store_sem.shape
+    span = rows_v.shape[1] // pieces
+    for n in range(pieces):
+        cols = pl.ds(n * span, span)
+        loads.append(
+            pltpu.make_async_copy(rows.at[:, cols], rows_v.at[:, cols], load_sem.at[2 + n])
+        )
     for load in loads:
         load.start()
-    for load in loads[:2]:
-        load.wait()
-    steps = store_sem.shape[0]
+    loads[0].wait()
     tall = hid_v.shape[0] // steps
     stores = []
-    for m in range(steps):
-        block = pl.ds(m * tall, tall)
-        out_v[block, :] = jnp.dot(
-            hid_v[block, :], rows_v[...], preferred_element_type=jnp.float32
-        ).astype(jnp.bfloat16)
-        store = pltpu.make_async_copy(
-            out_v.at[block, :], grad_weight.at[0, 0, block, :], store_sem.at[m]
-        )
-        store.start()
-        stores.append(store)
-        if m == 0:
-            loads[2].wait()
-            summed = shares_v[0].astype(jnp.float32)
-            for e in range(1, shares_v.shape[0]):
-                summed = summed + shares_v[e].astype(jnp.float32)
-            small_v[...] = summed.astype(jnp.bfloat16)
-            store = pltpu.make_async_copy(small_v, grad_hidden.at[0, 0], small_sem)
+    for n in range(pieces):
+        loads[2 + n].wait()
+        cols = pl.ds(n * span, span)
+        for m in range(steps):
+            block = pl.ds(m * tall, tall)
+            out_v[block, cols] = jnp.dot(
+                hid_v[block, :], rows_v[:, cols], preferred_element_type=jnp.float32
+            ).astype(jnp.bfloat16)
+            store = pltpu.make_async_copy(
+                out_v.at[block, cols], grad_weight.at[0, 0, block, cols], store_sem.at[n, m]
+            )
             store.start()
             stores.append(store)
+            if n == 0 and m == 0:
+                loads[1].wait()
+                summed = shares_v[0].astype(jnp.float32)
+                for e in range(1, shares_v.shape[0]):
+                    summed = summed + shares_v[e].astype(jnp.float32)
+                small_v[...] = summed.astype(jnp.bfloat16)
+                store = pltpu.make_async_copy(small_v, grad_hidden.at[0, 0], small_sem)
+                store.start()
+                stores.append(store)
     for store in stores:
         store.wait()
 
@@ -423,7 +430,7 @@
         ),
     )(grad_tokens, slot_token, send_count, route_score, hidden_act, w_down)
 
-    steps = 8
+    steps = 4
     return pl.pallas_call(
         weight_kernel,
         out_shape=(
@@ -438,9 +445,9 @@
             pltpu.VMEM((n_ep, own_rows, units), bf16),
             pltpu.VMEM((own_rows, units), bf16),
             pltpu.VMEM((half, width), bf16),
-            dma((3,)),
+            dma((2 + parts,)),
             dma,
-            dma((steps,)),
+            dma((parts, steps)),
         ],
         compiler_params=pltpu.CompilerParams(vmem_limit_bytes=63 * 2**20),
     )(hidden, rows, shares)

time: 27.6 us -> 27.6 us (level)
  no operation moved by 1% of the time
where the time goes in v4:
time: 27.6 us; the launch traced here: 27.4 us
  Pallas kernels  26.8 us (97%)
  between operations  0.64 us (2%)
    pallas_call x1, Pallas kernels, local(): pl.pallas_call(functools.partial(relay_kernel, sizes, parts), out_shape=(...  23.2 us
    pallas_call x1, Pallas kernels, local(): pl.pallas_call(weight_kernel, out_shape=(jax.ShapeDtypeStruct((1, 1, own_...  3.59 us

profile of v4, /device:TPU:0, one launch (start us, length us, event | category | flops | bytes accessed | tf_op | source)
XLA Modules:
  0.0 27.4 jit_solution(11555372445206499082)
XLA Ops:
  0.6 23.2 %shard_map.77 = (bf16[128,3584]{1,0:T(8,128)(2,1)}, bf16[512,128]{1,0:T(8,128)(2,1)}, bf16[2,32,1024]{2,1,0:T(8,128)(2,1)}) custom-call(bf16[1,1,1,128,7168]{4,3,2,1,0:T(8,128)(2,1)} %tokens.1, s32[1,1,1,4,8]{4,3,2,1,0:T(4,128)} %slots.1, s32[1,1,1,4]{3,2,1,0:T(1,128)} %counts.1, f32[1,1,1,4,8]{4,3,2,1,0:T(4,128)} %scores.1, ...), custom_call_target="tpu_custom_call" | custom-call | tf_op jit(solution)/shard_map/pallas_call | solution.py:387
  23.9 3.6 %shard_map.78 = (bf16[1,1,32,1024]{3,2,1,0:T(8,128)(2,1)}, bf16[1,1,512,3584]{3,2,1,0:T(8,128)(2,1)}) custom-call(bf16[512,128]{1,0:T(8,128)(2,1)} %get-tuple-element.5.hidden, bf16[128,3584]{1,0:T(8,128)(2,1)} %get-tuple-element.6.rows, bf16[2,32,1024]{2,1,0:T(8,128)(2,1)} %get-tuple-element.7.shares), custom_call_target="tpu_custom_call" | custom-call | tf_op jit(solution)/shard_map/pallas_call | solution.py:434
